TPU v7x, 32 devices: a whole 2x2x4 slice. The times are simulated.
32 devices in a mesh: row: 2 (over x), col: 4 (over z), depth: 4 (over y, core).
Axes of the slice: x: 2, y: 2, z: 4, core: 2. Of those that a mesh axis runs over, the one named last changes fastest.
Arguments:
- k_parts: bfloat16 [2, 1024, 1024], P(None, 'row', 'col'), as said below
- p_parts: bfloat16 [2, 1024, 1024], P(None, 'row', 'col'), as said below
- k_mask: int32 [16, 16], P('row', 'col'), may hold values from 0 to 1, as said below
- p_mask: int32 [16, 16], P('row', 'col'), may hold values from 0 to 1, as said below
- atoms: int32 [16], replicated, may hold values from 0 to 3, as said below
- classes: int32 [4, 4], replicated, may hold values from 0 to 3
- rates: float32 [4], replicated, may hold values from 0.5 to 8
Outputs:
- derivative: float32 [2, 1024, 1024], P(None, ('row', 'depth'), 'col')
Inputs may be any that keep to these rules, and one draw needn't show every extreme that they name: k_parts[0] is symmetric and k_parts[1] antisymmetric, so the Kohn-Sham matrix is Hermitian. p_parts[0] is symmetric and p_parts[1] antisymmetric, so the density matrix is Hermitian. `k_mask`: symmetric; every diagonal tile is kept; each tile row keeps a band of tiles around the diagonal of its own half-width, from 0 to 4 tiles, besides scattered tiles further away. `p_mask`: symmetric; every diagonal tile is kept; each tile row keeps a band of tiles around the diagonal of its own half-width, from 0 to 4 tiles, besides scattered tiles further away. `atoms`: never falling along the tiles; every atom block holds at least one tile.
All inputs are finite; a program needn't handle non-finite values.
Results may differ from a plain program's by a relative error of at most 0.0003.
Values may be sent and summed in bfloat16 or wider, within the bound.
No kernel may reach another device: no remote copies, remote signals or barrier semaphores. Data moves between devices by JAX's collectives and lax.ppermute only.
A program may use at most 64 MiB of HBM per device.

v0:
```python
import jax
import jax.numpy as jnp
from jax import lax
from jax.sharding import PartitionSpec as P

TILE = 64


def expand_mask(mask, tile, dtype):
    rows_t, cols_t = mask.shape
    grid = jnp.broadcast_to(mask[:, None, :, None], (rows_t, tile, cols_t, tile))
    return grid.reshape(rows_t * tile, cols_t * tile).astype(dtype)


def commute(k_rows, p_rows, k_cols, p_cols):
    left = jnp.concatenate((k_rows[0], k_rows[1], p_rows[0], p_rows[1]), axis=1)
    right = jnp.concatenate(
        (
            jnp.concatenate((p_cols[0], p_cols[1]), axis=1),
            jnp.concatenate((-p_cols[1], p_cols[0]), axis=1),
            jnp.concatenate((-k_cols[0], -k_cols[1]), axis=1),
            jnp.concatenate((k_cols[1], -k_cols[0]), axis=1),
        ),
        axis=0,
    )
    return jnp.dot(left, right, preferred_element_type=jnp.float32)


def make_fold(k_strip, p_strip, pieces):
    k_piece, p_piece = pieces
    return commute(k_strip, p_strip, k_piece, p_piece)


def body(k_parts, p_parts, k_mask, p_mask, atoms, classes, rates):
    k_local = k_parts * expand_mask(k_mask, TILE, jnp.bfloat16)[None]
    p_local = p_parts * expand_mask(p_mask, TILE, jnp.bfloat16)[None]
    rows_here = k_local.shape[1]
    cols_here = k_local.shape[2]
    depth = lax.axis_size("depth")
    layer = lax.axis_index("depth")
    out_rows = rows_here // depth
    k_strip = lax.dynamic_slice_in_dim(k_local, layer * out_rows, out_rows, 1)
    p_strip = lax.dynamic_slice_in_dim(p_local, layer * out_rows, out_rows, 1)
    k_strip, p_strip = (
        lax.all_gather(k_strip, "col", axis=2, tiled=True),
        lax.all_gather(p_strip, "col", axis=2, tiled=True),
    )
    total = make_fold(
        k_strip,
        p_strip,
        (
            lax.all_gather(k_local, "row", axis=1, tiled=True),
            lax.all_gather(p_local, "row", axis=1, tiled=True),
        ),
    )
    z_real = total[:, :cols_here]
    z_imag = total[:, cols_here:]
    grid_row = lax.axis_index("row") * depth + layer
    row_tiles = out_rows // TILE
    col_tiles = cols_here // TILE
    atom_rows = lax.dynamic_slice_in_dim(atoms, grid_row * row_tiles, row_tiles)
    atom_cols = lax.dynamic_slice_in_dim(atoms, lax.axis_index("col") * col_tiles, col_tiles)
    blocks = classes.shape[0]
    levels = rates.shape[0]
    block_ids = jnp.arange(blocks, dtype=jnp.int32)
    hot_rows = (atom_rows[:, None] == block_ids[None, :]).astype(jnp.float32)
    hot_cols = (atom_cols[:, None] == block_ids[None, :]).astype(jnp.float32)
    kinds = jnp.dot(
        jnp.dot(hot_rows, classes.astype(jnp.float32), precision=lax.Precision.HIGHEST),
        hot_cols.T,
        precision=lax.Precision.HIGHEST,
    )
    level_ids = jnp.arange(levels, dtype=jnp.float32)
    tile_rate = jnp.sum(
        (kinds[:, :, None] == level_ids[None, None, :]).astype(jnp.float32) * rates[None, None, :],
        axis=2,
    )
    differ = (atom_rows[:, None] != atom_cols[None, :]).astype(jnp.float32)
    tile_rate = tile_rate * differ
    gamma = expand_mask(tile_rate, TILE, jnp.float32)
    p_rows_out = lax.dynamic_slice_in_dim(p_local, layer * out_rows, out_rows, 1).astype(
        jnp.float32
    )
    real_out = z_imag - gamma * p_rows_out[0]
    imag_out = -z_real - gamma * p_rows_out[1]
    return jnp.stack((real_out, imag_out))


def solution(mesh):
    return jax.shard_map(
        body,
        mesh=mesh,
        in_specs=(
            P(None, "row", "col"),
            P(None, "row", "col"),
            P("row", "col"),
            P("row", "col"),
            P(),
            P(),
            P(),
        ),
        out_specs=P(None, ("row", "depth"), "col"),
        check_vma=False,
    )
```

profile of v0, /device:TPU:0, one launch (start us, length us, event | category | flops | bytes accessed | tf_op | source)
XLA Modules:
  0.0 65.9 jit_solution(6025978454134886618)
XLA Ops:
  6.5 0.0 copy-start.2
  6.5 0.0 all-gather.5.cloned.1.call-start
  6.5 0.7 %convert_element_type.32 = bf16[8,4]{0,1:T(4,128)(2,1)S(1)} convert(s32[8,4]{0,1:T(4,128)} %param.9) | non-fusion elementwise | flops 32 | bytes 192 | tf_op jit(solution)/shard_map/convert_element_type | solution.py:12
  7.3 0.1 copy.10
  7.4 0.2 broadcast_in_dim.6
  7.6 0.3 convert_element_type.33
  7.9 0.0 copy-done.2
  7.9 0.0 copy-start.4
  8.0 0.9 %broadcast_multiply_fusion.1 = bf16[2,512,256]{2,1,0:T(8,128)(2,1)} fusion(bf16[2,512,256]{2,1,0:T(8,128)(2,1)S(1)} %copy-done.2, bf16[512,256]{1,0:T(8,128)(2,1)S(1)} %convert_element_type.33), kind=kLoop, calls=%fused_computation.34 | loop fusion | flops 262144 | bytes 1310720 | tf_op jit(solution)/shard_map/mul | solution.py:35
  8.8 0.0 copy-start.3
  8.8 0.0 all-gather.5.cloned.1.call-update
  8.8 0.0 all-gather.3.cloned.1.call-start
  8.9 0.0 copy-done.4
  8.9 0.1 copy.11
  9.0 0.2 broadcast_in_dim.7
  9.2 0.3 convert_element_type.35
  9.6 0.3 copy-done.3
  9.9 0.0 copy-start.7
  9.9 0.0 copy-start.6
  9.9 0.9 %broadcast_multiply_fusion = bf16[2,512,256]{2,1,0:T(8,128)(2,1)} fusion(bf16[2,512,256]{2,1,0:T(8,128)(2,1)S(1)} %copy-done.3, bf16[512,256]{1,0:T(8,128)(2,1)S(1)} %convert_element_type.35), kind=kLoop, calls=%fused_computation.33 | loop fusion | flops 262144 | bytes 1310720 | tf_op jit(solution)/shard_map/mul | solution.py:36
  10.7 0.0 copy-start.5
  10.7 0.0 all-gather.3.cloned.1.call-update
  10.8 0.9 %fusion.40 = (f32[2,128,256]{2,1,0:T(8,128)S(1)}, bf16[2,128,256]{2,1,0:T(8,128)(2,1)S(1)}) fusion(bf16[2,512,256]{2,1,0:T(8,128)(2,1)} %broadcast_multiply_fusion, s32[]{:T(128)S(6)} %select_n.11), kind=kLoop, calls=%fused_computation.60 | loop fusion | flops 65536 | bytes 524292 | tf_op jit(solution)/shard_map/convert_element_type | solution.py:81
  11.7 0.9 %constant_dynamic-slice_fusion.1 = bf16[2,128,256]{2,1,0:T(8,128)(2,1)S(1)} fusion(bf16[2,512,256]{2,1,0:T(8,128)(2,1)} %broadcast_multiply_fusion.1, s32[]{:T(128)S(6)} %select_n.11), kind=kLoop, calls=%fused_computation.55 | loop fusion | bytes 262148 | tf_op jit(solution)/shard_map/dynamic_slice | solution.py:42
  12.6 0.0 copy-done.7
  12.6 0.1 dynamic_slice.15
  12.7 0.1 dynamic_slice.16
  12.8 0.0 copy-done.6
  12.8 0.2 fusion.30
  13.0 0.2 fusion.33
  13.2 0.0 copy-done.5
  13.2 0.2 select_reduce_fusion
  13.3 0.1 compare_select_fusion
  13.4 17.3 %all_gather.13 = bf16[2,128,1024]{2,1,0:T(8,128)(2,1)S(1)} all-gather(bf16[2,128,256]{2,1,0:T(8,128)(2,1)S(1)} %get-tuple-element.6), channel_id=1, replica_groups=mesh['row'=2,'col'=4,'depth'=4] {'col'}, dimensions={2}, use_global_device_ids=true | all-gather | bytes 655360 | tf_op jit(solution)/shard_map/all_gather | solution.py:46
  30.8 16.2 %all_gather.12 = bf16[2,128,1024]{2,1,0:T(8,128)(2,1)S(1)} all-gather(bf16[2,128,256]{2,1,0:T(8,128)(2,1)S(1)} %constant_dynamic-slice_fusion.1), channel_id=1, replica_groups=mesh['row'=2,'col'=4,'depth'=4] {'col'}, dimensions={2}, use_global_device_ids=true | all-gather | bytes 655360 | tf_op jit(solution)/shard_map/all_gather | solution.py:45
  46.9 0.1 broadcast_in_dim.8
  47.0 0.2 reshape.52
  47.3 0.0 all-gather.5.cloned.1.call-done
  47.3 0.0 copy-start
  47.4 1.2 %fusion.39 = bf16[1024,256]{1,0:T(8,128)(2,1)S(1)} fusion(bf16[2,1024,256]{2,1,0:T(8,128)(2,1)} %all-gather.5.cloned.1.call-done), kind=kLoop, calls=%fused_computation.59 | loop fusion | flops 262144 | bytes 1048576 | tf_op jit(solution)/shard_map/neg | solution.py:21
  48.5 0.2 copy-done
  48.7 0.1 slice_bitcast_fusion
  48.8 7.1 %all-gather.3.cloned.1.call-done = bf16[2,1024,256]{2,1,0:T(8,128)(2,1)} async-done(((bf16[2,512,256]{2,1,0:T(8,128)(2,1)}), bf16[2,1024,256]{2,1,0:T(8,128)(2,1)}) %all-gather.3.cloned.1.call-update) | async-done | bytes 1048592 | tf_op jit(solution)/shard_map/all_gather | solution.py:53
  55.9 1.4 %slice_bitcast_fusion.1 = (bf16[1024,256]{1,0:T(8,128)(2,1)S(1)}, bf16[1024,256]{1,0:T(8,128)(2,1)S(1)}) fusion(bf16[2,1024,256]{2,1,0:T(8,128)(2,1)} %all-gather.3.cloned.1.call-done), kind=kLoop, calls=%fused_computation.26 | loop fusion | bytes 2097152 | tf_op jit(solution)/shard_map/squeeze | solution.py:19
  57.2 0.2 copy-done.1
  57.5 0.8 %fusion = f32[128,512]{1,0:T(8,128)S(1)} fusion(bf16[1024,256]{1,0:T(8,128)(2,1)S(1)} %get-tuple-element.10, bf16[1024,256]{1,0:T(8,128)(2,1)S(1)} %get-tuple-element.9, bf16[1024,256]{1,0:T(8,128)(2,1)S(1)} %fusion.39, bf16[1024,256]{1,0:T(8,128)(2,1)S(1)} %get-tuple-element.8, bf16[1024,256]{1,0:T(8,128)(2,1)S(1)} %fusion.38, ...), kind=kOutput, calls=%fused_computation | convolution fusion | flops 574619648 | bytes 4456448 | tf_op jit(solution)/shard_map/dot_general | solution.py:26
  58.2 0.1 fusion.29
  58.3 0.7 %pad_maximum_fusion = f32[2,128,256]{2,1,0:T(8,128)} fusion(f32[1,128,256]{2,1,0:T(8,128)S(1)} %get-tuple-element.12, f32[1,128,256]{2,1,0:T(8,128)S(1)} %get-tuple-element.11), kind=kLoop, calls=%fused_computation.32 | loop fusion | flops 65536 | bytes 524288 | tf_op jit(solution)/shard_map/stack | solution.py:86
  (5 shorter events, 0.1 us)
Async XLA Ops:
  6.5 1.4 %copy-start.2 = (bf16[2,512,256]{2,1,0:T(8,128)(2,1)S(1)}, bf16[2,512,256]{2,1,0:T(8,128)(2,1)}, u32[]{:S(2)}) copy-start(bf16[2,512,256]{2,1,0:T(8,128)(2,1)} %param.7) | copy-start | bytes 1572868
  6.5 40.8 %all-gather.5.cloned.1.call-start = ((), (), s32[]{:S(2)}) async-start(), calls=%async_computation.1 | async-start | bytes 1572864 | tf_op jit(solution)/shard_map/all_gather | solution.py:52
  7.9 0.9 %copy-start.4 = (s32[8,4]{0,1:T(4,128)S(1)}, s32[8,4]{0,1:T(4,128)}, u32[]{:S(2)}) copy-start(s32[8,4]{0,1:T(4,128)} %param.10) | copy-start | bytes 388
  8.8 1.0 %copy-start.3 = (bf16[2,512,256]{2,1,0:T(8,128)(2,1)S(1)}, bf16[2,512,256]{2,1,0:T(8,128)(2,1)}, u32[]{:S(2)}) copy-start(bf16[2,512,256]{2,1,0:T(8,128)(2,1)} %param.8) | copy-start | bytes 1572868
  8.8 47.0 %all-gather.3.cloned.1.call-start = ((), (), s32[]{:S(2)}) async-start(), calls=%async_computation | async-start | bytes 1572864 | tf_op jit(solution)/shard_map/all_gather | solution.py:53
  9.9 2.8 %copy-start.7 = (s32[16]{0:T(128)S(1)}, s32[16]{0:T(128)}, u32[]{:S(2)}) copy-start(s32[16]{0:T(128)} %param.11) | copy-start | bytes 196
  9.9 2.9 %copy-start.6 = (s32[4,4]{1,0:T(4,128)S(1)}, s32[4,4]{1,0:T(4,128)}, u32[]{:S(2)}) copy-start(s32[4,4]{1,0:T(4,128)} %param.12) | copy-start | bytes 196
  10.7 2.5 %copy-start.5 = (f32[4]{0:T(128)S(1)}, f32[4]{0:T(128)}, u32[]{:S(2)}) copy-start(f32[4]{0:T(128)} %param.13) | copy-start | bytes 52
  47.3 1.4 %copy-start = (bf16[2,1024,256]{2,1,0:T(8,128)(2,1)S(1)}, bf16[2,1024,256]{2,1,0:T(8,128)(2,1)}, u32[]{:S(2)}) copy-start(bf16[2,1024,256]{2,1,0:T(8,128)(2,1)} %all-gather.5.cloned.1.call-done) | copy-start | bytes 3145732
  55.9 1.5 %copy-start.1 = (bf16[2,1024,256]{2,1,0:T(8,128)(2,1)S(1)}, bf16[2,1024,256]{2,1,0:T(8,128)(2,1)}, u32[]{:S(2)}) copy-start(bf16[2,1024,256]{2,1,0:T(8,128)(2,1)} %all-gather.3.cloned.1.call-done) | copy-start | bytes 3145732
Sparse Core Ops, SparseCore 0:
  9.0 23.9 all-gather.4
  34.5 21.2 all-gather.2
where the time goes:
time: 66.1 us; the launch traced here: 65.9 us
  blocking collectives  33.5 us (51%)
  between operations  13.6 us (21%)
  waiting for transfers between devices  7.13 us (11%)
  other arithmetic  5.71 us (9%)
  local copies, waits for them, and re-layouts  4.78 us (7%)
  matrix products  1.14 us (2%)
    all_gather x1, blocking collectives, body(): lax.all_gather(p_strip, 'col', axis=2, tiled=True)  17.3 us
    all_gather x1, blocking collectives, body(): lax.all_gather(k_strip, 'col', axis=2, tiled=True)  16.2 us
    all_gather x1, waiting for transfers between devices, body(): lax.all_gather(p_local, 'row', axis=1, tiled=True)  7.08 us
    squeeze x1, local copies, waits for them, and re-layouts, commute(): p_cols[1]  1.36 us
  transfers between devices with their start and end apart: 2, of which 1 were waited for; matrix products, arithmetic and copies ran while one was open for 9% of the time, Pallas kernels for 0%

commit v1 on v0

v1 whole, which is shorter than its diff:
```python
import functools

import jax
import jax.numpy as jnp
from jax import lax
from jax.experimental import pallas as pl
from jax.experimental.pallas import tpu as pltpu
from jax.sharding import PartitionSpec as P

TILE = 64


def tile_row(mask_ref, tile, width, dtype):
    lanes = lax.broadcasted_iota(jnp.int32, (1, width), 1) // TILE
    row = jnp.zeros((1, width), jnp.float32)
    for place in range(width // TILE):
        row = jnp.where(lanes == place, mask_ref[tile, place].astype(jnp.float32), row)
    return row.astype(dtype)


def strip_kernel(place, k_mask, p_mask, k_ref, p_ref, out_ref):
    rows, width = k_ref.shape[1:]
    tiles = rows // TILE
    for tile in range(tiles):
        span = pl.ds(tile * TILE, TILE)
        for slot, mask_ref, ref in ((0, k_mask, k_ref), (2, p_mask, p_ref)):
            row = tile_row(mask_ref, place[2] * tiles + tile, width, ref.dtype)
            for part in range(2):
                out_ref[slot + part, span, :] = ref[part, span, :] * row


def mask_strip(place, k_mask, p_mask, k_parts, p_parts, out_rows):
    width = k_parts.shape[2]
    block = pl.BlockSpec((2, out_rows, width), lambda g, place, km, pm: (0, place[2], 0))
    return pl.pallas_call(
        strip_kernel,
        grid_spec=pltpu.PrefetchScalarGridSpec(
            num_scalar_prefetch=3,
            grid=(1,),
            in_specs=[block, block],
            out_specs=pl.BlockSpec((4, out_rows, width), lambda g, *_: (0, 0, 0)),
        ),
        out_shape=jax.ShapeDtypeStruct((4, out_rows, width), k_parts.dtype),
        name="mask_strip",
    )(place, k_mask, p_mask, k_parts, p_parts)


def product_kernel(
    rows_n, cols_n, depth, place, k_mask, p_mask, atoms, classes, rates, k_ref, p_ref, *refs
):
    row_strips = refs[:cols_n]
    col_strips = refs[cols_n : cols_n + (rows_n - 1) * depth]
    out_ref, left, right = refs[cols_n + (rows_n - 1) * depth :]
    out_rows, width = row_strips[0].shape[1:]
    here = k_ref.shape[1]
    row, col, layer = place[0], place[1], place[2]
    own = row_strips[0]
    for shift, ref in enumerate(row_strips):
        at = pl.ds(pl.multiple_of(lax.rem(col - shift + cols_n, cols_n) * width, width), width)
        k_re, k_im, p_re, p_im = ref[0], ref[1], ref[2], ref[3]
        top, low = pl.ds(0, out_rows), pl.ds(out_rows, out_rows)
        left[0, top, at] = k_re
        left[0, low, at] = k_im
        left[1, top, at] = -k_im
        left[1, low, at] = k_re
        left[2, top, at] = -p_re
        left[2, low, at] = -p_im
        left[3, top, at] = p_im
        left[3, low, at] = -p_re
    for tile in range(here // TILE):
        span = pl.ds(tile * TILE, TILE)
        at = pl.ds(pl.multiple_of(row * here + tile * TILE, TILE), TILE)
        for slot, mask_ref, ref in ((2, k_mask, k_ref), (0, p_mask, p_ref)):
            factor = tile_row(mask_ref, tile, width, ref.dtype)
            for part in range(2):
                right[slot + part, at, :] = ref[part, span, :] * factor
    for index, ref in enumerate(col_strips):
        shift, flip = index // depth + 1, index % depth
        start = lax.rem(row - shift + rows_n, rows_n) * here + (layer ^ flip) * out_rows
        at = pl.ds(pl.multiple_of(start, out_rows), out_rows)
        right[2, at, :] = ref[0]
        right[3, at, :] = ref[1]
        right[0, at, :] = ref[2]
        right[1, at, :] = ref[3]
    total = jnp.zeros((2 * out_rows, width), jnp.float32)
    for slot in range(4):
        total += jnp.dot(left[slot], right[slot], preferred_element_type=jnp.float32)
    z_re, z_im = total[:out_rows], total[out_rows:]
    lanes = lax.broadcasted_iota(jnp.int32, (1, width), 1) // TILE
    row_tiles, col_tiles = out_rows // TILE, width // TILE
    for tile in range(row_tiles):
        span = pl.ds(tile * TILE, TILE)
        atom_row = atoms[(row * depth + layer) * row_tiles + tile]
        gamma = jnp.zeros((1, width), jnp.float32)
        for spot in range(col_tiles):
            atom_col = atoms[col * col_tiles + spot]
            rate = jnp.where(atom_row != atom_col, rates[classes[atom_row, atom_col]], 0.0)
            gamma = jnp.where(lanes == spot, rate, gamma)
        cut = slice(tile * TILE, (tile + 1) * TILE)
        out_ref[0, span, :] = z_im[cut] - gamma * own[2, span, :].astype(jnp.float32)
        out_ref[1, span, :] = -z_re[cut] - gamma * own[3, span, :].astype(jnp.float32)


def exchange(x, axis, perm):
    return lax.ppermute(x, axis, perm)


def body(k_parts, p_parts, k_mask, p_mask, atoms, classes, rates):
    rows_n, cols_n, depth = (lax.axis_size(a) for a in ("row", "col", "depth"))
    place = jnp.stack([lax.axis_index(a) for a in ("row", "col", "depth")]).astype(jnp.int32)
    here, width = k_parts.shape[1:]
    out_rows = here // depth
    strip = mask_strip(place, k_mask, p_mask, k_parts, p_parts, out_rows)
    col_strips = []
    for shift in range(1, rows_n):
        pieces = {0: exchange(strip, "row", [(i, (i + shift) % rows_n) for i in range(rows_n)])}
        stride = depth // 2
        while stride:
            perm = [(i, i ^ stride) for i in range(depth)]
            for flip in list(pieces):
                pieces[flip ^ stride] = exchange(pieces[flip], "depth", perm)
            stride //= 2
        col_strips += [pieces[flip] for flip in range(depth)]
    row_strips = [strip]
    for shift in range(1, cols_n):
        row_strips.append(
            exchange(strip, "col", [(i, (i + shift) % cols_n) for i in range(cols_n)])
        )
    total_rows = here * rows_n
    need = 2 * (4 * total_rows * width * 2 + 12 * out_rows * total_rows * 2 + 4 * here * width * 2)
    smem = pl.BlockSpec(memory_space=pltpu.SMEM)
    vmem = pl.BlockSpec(memory_space=pltpu.VMEM)
    n_vec = 2 + len(row_strips) + len(col_strips)
    return pl.pallas_call(
        functools.partial(product_kernel, rows_n, cols_n, depth),
        in_specs=[smem] * 6 + [vmem] * n_vec,
        out_specs=vmem,
        out_shape=jax.ShapeDtypeStruct((2, out_rows, width), jnp.float32),
        scratch_shapes=[
            pltpu.VMEM((4, 2 * out_rows, total_rows), k_parts.dtype),
            pltpu.VMEM((4, total_rows, width), k_parts.dtype),
        ],
        compiler_params=pltpu.CompilerParams(vmem_limit_bytes=need + (4 << 20)),
        name="commutator",
    )(place, k_mask, p_mask, atoms, classes, rates, k_parts, p_parts, *row_strips, *col_strips)


def solution(mesh):
    return jax.shard_map(
        body,
        mesh=mesh,
        in_specs=(
            P(None, "row", "col"),
            P(None, "row", "col"),
            P("row", "col"),
            P("row", "col"),
            P(),
            P(),
            P(),
        ),
        out_specs=P(None, ("row", "depth"), "col"),
        check_vma=False,
    )
```

time: 66.1 us -> 45.3 us (0.69)
  blocking collectives: 33.5 us -> 0 us
  waiting for transfers between devices: 7.13 us -> 26.9 us
  between operations: 13.6 us -> 0.12 us
  starting transfers between devices: 0.04 us -> 9.33 us
  Pallas kernels: 0 us -> 5.18 us
  other arithmetic: 5.71 us -> 0.6 us
  local copies, waits for them, and re-layouts: 4.78 us -> 3.01 us
  matrix products: 1.14 us -> 0 us
    all_gather x2 -> x0, blocking collectives: 33.5 us -> none  [the longest x1 17.3 us: body(): lax.all_gather(p_strip, 'col', axis=2, tiled=True)]
    ppermute x0 -> x7, waiting for transfers between devices: none -> 26.9 us  [exchange(): return lax.ppermute(x, axis, perm)]
    ppermute x0 -> x7, starting transfers between devices: none -> 9.33 us  [exchange(): return lax.ppermute(x, axis, perm)]
    all_gather x2 -> x0, waiting for transfers between devices: 7.1 us -> none  [the longest x1 7.08 us: body(): lax.all_gather(p_local, 'row', axis=1, tiled=True)]
    pallas_call x0 -> x2, Pallas kernels: none -> 5.18 us  [the longest x1 2.63 us: mask_strip(): pl.pallas_call(strip_kernel, grid_spec=pltpu.PrefetchScalarGridSpec(num_s...]
    unnamed x16 -> x24, local copies, waits for them, and re-layouts: 0.7 us -> 3.01 us
    mul x3 -> x0, other arithmetic: 1.79 us -> none  [the longest x1 0.86 us: body(): p_local = p_parts * expand_mask(p_mask, TILE, jnp.bfloat16)[None]]
    convert_element_type x3 -> x0, other arithmetic: 1.69 us -> none  [the longest x1 0.94 us: body(): lax.dynamic_slice_in_dim(p_local, layer * out_rows, out_rows, 1)]
  transfers between devices with their start and end apart: 2 -> 7, of which waited for: 1 -> 4; matrix products, arithmetic and copies ran while one was open for 9% -> 0% of each run, Pallas kernels for 0% -> 0%
where the time goes in v1:
time: 45.3 us; the launch traced here: 45.1 us
  waiting for transfers between devices  26.9 us (59%)
  starting transfers between devices  9.33 us (21%)
  Pallas kernels  5.18 us (11%)
  local copies, waits for them, and re-layouts  3.01 us (7%)
  other arithmetic  0.6 us (1%)
    ppermute x7, waiting for transfers between devices, exchange(): return lax.ppermute(x, axis, perm)  26.9 us
    ppermute x7, starting transfers between devices, exchange(): return lax.ppermute(x, axis, perm)  9.33 us
    unnamed x24, local copies, waits for them, and re-layouts  3.01 us
    pallas_call x1, Pallas kernels, mask_strip(): pl.pallas_call(strip_kernel, grid_spec=pltpu.PrefetchScalarGridSpec(num_s...  2.63 us
    pallas_call x1, Pallas kernels, body(): pl.pallas_call(functools.partial(product_kernel, rows_n, cols_n, depth),...  2.54 us
  transfers between devices with their start and end apart: 7, of which 4 were waited for; matrix products, arithmetic and copies ran while one was open for 0% of the time, Pallas kernels for 0%

profile of v1, /device:TPU:0, one launch (start us, length us, event | category | flops | bytes accessed | tf_op | source)
XLA Modules:
  0.0 45.1 jit_solution(1595944755660743870)
XLA Ops:
  0.0 0.0 copy-start.9
  0.0 0.7 %copy-done.9 = s32[8,4]{0,1:T(4,128)S(1)} copy-done((s32[8,4]{0,1:T(4,128)S(1)}, s32[8,4]{0,1:T(4,128)}, u32[]{:S(2)}) %copy-start.9) | copy-done | bytes 152
  0.7 0.0 copy-start.10
  0.7 0.7 %copy.10.k_mask = s32[8,4]{1,0:T(8,128)} copy(s32[8,4]{0,1:T(4,128)S(1)} %copy-done.9) | data formatting | bytes 256 | tf_op args[2]
  1.4 0.0 copy-done.10
  1.4 0.7 %copy.11.p_mask = s32[8,4]{1,0:T(8,128)} copy(s32[8,4]{0,1:T(4,128)S(1)} %copy-done.10) | data formatting | bytes 256 | tf_op args[3]
  2.0 0.6 %pad_add_fusion.place = s32[3]{0:T(128)} fusion(s32[1]{0:T(128)} %bitcast.2, s32[1]{0:T(128)} %bitcast.1, s32[1]{0:T(128)} %bitcast), kind=kLoop, calls=%fused_computation | loop fusion | flops 6 | bytes 24 | tf_op jit(solution)/shard_map/stack | solution.py:110
  2.6 0.0 copy-start
  2.6 0.0 copy-start.1
  2.6 0.0 copy-start.3
  2.6 0.0 copy-start.4
  2.6 0.0 copy-start.5
  2.7 0.0 copy-start.6
  2.7 0.0 copy-start.7
  2.7 0.0 copy-start.8
  2.7 2.6 %mask_strip.1.refs_0_ = bf16[4,128,256]{2,1,0:T(8,128)(2,1)} custom-call(s32[3]{0:T(128)} %pad_add_fusion.place, s32[8,4]{1,0:T(8,128)} %copy.10.k_mask, s32[8,4]{1,0:T(8,128)} %copy.11.p_mask, bf16[2,512,256]{2,1,0:T(8,128)(2,1)} %k_ref.3, bf16[2,512,256]{2,1,0:T(8,128)(2,1)} %p_ref.3), custom_call_target="tpu_custom_call" | custom-call | tf_op jit(solution)/shard_map/mask_strip/pallas_call | solution.py:35
  5.3 2.9 %collective-permute-start.3 = (bf16[4,128,256]{2,1,0:T(8,128)(2,1)}, bf16[4,128,256]{2,1,0:T(8,128)(2,1)S(1)}, u32[]{:S(2)}, u32[]{:S(2)}) collective-permute-start(bf16[4,128,256]{2,1,0:T(8,128)(2,1)} %mask_strip.1.refs_0_), channel_id=1, source_target_pairs={{0,16},{16,0},{1,17},{17,1},{2,18},{18,2},{3,19},{19,3},{4,20},{20... | collective-permute-start | bytes 786440 | tf_op jit(solution)/shard_map/ppermute | solution.py:105
  8.3 6.5 %collective-permute-done.3.refs_4_ = bf16[4,128,256]{2,1,0:T(8,128)(2,1)S(1)} collective-permute-done((bf16[4,128,256]{2,1,0:T(8,128)(2,1)}, bf16[4,128,256]{2,1,0:T(8,128)(2,1)S(1)}, u32[]{:S(2)}, u32[]{:S(2)}) %collective-permute-start.3) | collective-permute-done | bytes 262176 | tf_op jit(solution)/shard_map/ppermute | solution.py:105
  14.8 1.8 %collective-permute-start.5 = (bf16[4,128,256]{2,1,0:T(8,128)(2,1)S(1)}, bf16[4,128,256]{2,1,0:T(8,128)(2,1)S(1)}, u32[]{:S(2)}, u32[]{:S(2)}) collective-permute-start(bf16[4,128,256]{2,1,0:T(8,128)(2,1)S(1)} %collective-permute-done.3.refs_4_), channel_id=1, source_target_pairs={{0,2},{1,3},{2,0},{3,1},{4,6},{5,7},{6,4},{7,5},{8,10},{9,11},{10,... | collective-permute-start | bytes 786440 | tf_op jit(solution)/shard_map/ppermute | solution.py:105
  16.6 3.6 %collective-permute-start.2 = (bf16[4,128,256]{2,1,0:T(8,128)(2,1)}, bf16[4,128,256]{2,1,0:T(8,128)(2,1)S(1)}, u32[]{:S(2)}, u32[]{:S(2)}) collective-permute-start(bf16[4,128,256]{2,1,0:T(8,128)(2,1)} %mask_strip.1.refs_0_), channel_id=1, source_target_pairs={{0,12},{4,0},{8,4},{12,8},{1,13},{5,1},{9,5},{13,9},{2,14},{6,2},{... | collective-permute-start | bytes 786440 | tf_op jit(solution)/shard_map/ppermute | solution.py:105
  20.2 0.0 collective-permute-start.1
  20.2 1.0 %collective-permute-start = (bf16[4,128,256]{2,1,0:T(8,128)(2,1)}, bf16[4,128,256]{2,1,0:T(8,128)(2,1)S(1)}, u32[]{:S(2)}, u32[]{:S(2)}) collective-permute-start(bf16[4,128,256]{2,1,0:T(8,128)(2,1)} %mask_strip.1.refs_0_), channel_id=1, source_target_pairs={{0,4},{4,8},{8,12},{12,0},{1,5},{5,9},{9,13},{13,1},{2,6},{6,10},{... | collective-permute-start | bytes 786440 | tf_op jit(solution)/shard_map/ppermute | solution.py:105
  21.2 0.0 collective-permute-start.4
  21.2 1.1 %collective-permute-done.5.refs_6_ = bf16[4,128,256]{2,1,0:T(8,128)(2,1)S(1)} collective-permute-done((bf16[4,128,256]{2,1,0:T(8,128)(2,1)S(1)}, bf16[4,128,256]{2,1,0:T(8,128)(2,1)S(1)}, u32[]{:S(2)}, u32[]{:S(2)}) %collective-permute-start.5) | collective-permute-done | bytes 262176 | tf_op jit(solution)/shard_map/ppermute | solution.py:105
  22.3 0.0 collective-permute-start.6
  22.3 5.0 %collective-permute-done.2.refs_3_ = bf16[4,128,256]{2,1,0:T(8,128)(2,1)S(1)} collective-permute-done((bf16[4,128,256]{2,1,0:T(8,128)(2,1)}, bf16[4,128,256]{2,1,0:T(8,128)(2,1)S(1)}, u32[]{:S(2)}, u32[]{:S(2)}) %collective-permute-start.2) | collective-permute-done | bytes 262176 | tf_op jit(solution)/shard_map/ppermute | solution.py:105
  27.3 14.2 %collective-permute-done.1.refs_2_ = bf16[4,128,256]{2,1,0:T(8,128)(2,1)S(1)} collective-permute-done((bf16[4,128,256]{2,1,0:T(8,128)(2,1)}, bf16[4,128,256]{2,1,0:T(8,128)(2,1)S(1)}, u32[]{:S(2)}, u32[]{:S(2)}) %collective-permute-start.1) | collective-permute-done | bytes 262176 | tf_op jit(solution)/shard_map/ppermute | solution.py:105
  41.5 0.0 collective-permute-done.refs_1_
  41.5 0.0 collective-permute-done.4.refs_5_
  41.5 0.0 collective-permute-done.6.refs_7_
  41.5 0.0 copy-done
  41.5 0.0 copy-done.1
  41.6 0.0 copy-done.3
  41.6 0.0 copy-done.4
  41.6 0.0 copy-done.5
  41.6 0.0 copy-done.6
  41.6 0.0 copy-done.7
  41.6 0.0 copy-done.8
  41.6 0.0 copy-start.2
  41.6 0.9 %copy-done.2 = bf16[4,128,256]{2,1,0:T(8,128)(2,1)S(1)} copy-done((bf16[4,128,256]{2,1,0:T(8,128)(2,1)S(1)}, bf16[4,128,256]{2,1,0:T(8,128)(2,1)}, u32[]{:S(2)}) %copy-start.2) | copy-done | bytes 262168
  42.6 2.5 %commutator.1 = f32[2,128,256]{2,1,0:T(8,128)} custom-call(s32[3]{0:T(128)S(1)} %copy-done.5, s32[8,4]{1,0:T(8,128)S(1)} %copy-done.3, s32[8,4]{1,0:T(8,128)S(1)} %copy-done.4, s32[16]{0:T(128)S(1)} %copy-done.7, s32[4,4]{1,0:T(4,128)S(1)} %copy-done.6, f32[4]{0:T(128)S(1)} %copy-done.8, bf16[2,512,256]{2,1,0:T(8,128)(2,1)S(1)} %copy-done, ...), custom_call_target="tpu_custom_call" | custom-call | tf_op jit(solution)/shard_map/commutator/pallas_call | solution.py:134
Async XLA Ops:
  0.0 0.7 %copy-start.9 = (s32[8,4]{0,1:T(4,128)S(1)}, s32[8,4]{0,1:T(4,128)}, u32[]{:S(2)}) copy-start(s32[8,4]{0,1:T(4,128)} %param.9) | copy-start | bytes 388
  0.7 0.7 %copy-start.10 = (s32[8,4]{0,1:T(4,128)S(1)}, s32[8,4]{0,1:T(4,128)}, u32[]{:S(2)}) copy-start(s32[8,4]{0,1:T(4,128)} %param.10) | copy-start | bytes 388
  2.6 38.9 %copy-start = (bf16[2,512,256]{2,1,0:T(8,128)(2,1)S(1)}, bf16[2,512,256]{2,1,0:T(8,128)(2,1)}, u32[]{:S(2)}) copy-start(bf16[2,512,256]{2,1,0:T(8,128)(2,1)} %k_ref.3) | copy-start | bytes 1572868
  2.6 38.9 %copy-start.1 = (bf16[2,512,256]{2,1,0:T(8,128)(2,1)S(1)}, bf16[2,512,256]{2,1,0:T(8,128)(2,1)}, u32[]{:S(2)}) copy-start(bf16[2,512,256]{2,1,0:T(8,128)(2,1)} %p_ref.3) | copy-start | bytes 1572868
  2.6 38.9 %copy-start.3 = (s32[8,4]{1,0:T(8,128)S(1)}, s32[8,4]{1,0:T(8,128)}, u32[]{:S(2)}) copy-start(s32[8,4]{1,0:T(8,128)} %copy.10.k_mask) | copy-start | bytes 388
  2.6 38.9 %copy-start.4 = (s32[8,4]{1,0:T(8,128)S(1)}, s32[8,4]{1,0:T(8,128)}, u32[]{:S(2)}) copy-start(s32[8,4]{1,0:T(8,128)} %copy.11.p_mask) | copy-start | bytes 388
  2.6 38.9 %copy-start.5 = (s32[3]{0:T(128)S(1)}, s32[3]{0:T(128)}, u32[]{:S(2)}) copy-start(s32[3]{0:T(128)} %pad_add_fusion.place) | copy-start | bytes 40
  2.7 38.9 %copy-start.6 = (s32[4,4]{1,0:T(4,128)S(1)}, s32[4,4]{1,0:T(4,128)}, u32[]{:S(2)}) copy-start(s32[4,4]{1,0:T(4,128)} %classes.1) | copy-start | bytes 196
  2.7 38.9 %copy-start.7 = (s32[16]{0:T(128)S(1)}, s32[16]{0:T(128)}, u32[]{:S(2)}) copy-start(s32[16]{0:T(128)} %atoms.1) | copy-start | bytes 196
  2.7 38.9 %copy-start.8 = (f32[4]{0:T(128)S(1)}, f32[4]{0:T(128)}, u32[]{:S(2)}) copy-start(f32[4]{0:T(128)} %rates.1) | copy-start | bytes 52
  5.3 9.5 %collective-permute-start.3 = (bf16[4,128,256]{2,1,0:T(8,128)(2,1)}, bf16[4,128,256]{2,1,0:T(8,128)(2,1)S(1)}, u32[]{:S(2)}, u32[]{:S(2)}) collective-permute-start(bf16[4,128,256]{2,1,0:T(8,128)(2,1)} %mask_strip.1.refs_0_), channel_id=1, source_target_pairs={{0,16},{16,0},{1,17},{17,1},{2,18},{18,2},{3,19},{19,3},{4,20},{20... | collective-permute-start | bytes 786440 | tf_op jit(solution)/shard_map/ppermute | solution.py:105
  14.8 7.5 %collective-permute-start.5 = (bf16[4,128,256]{2,1,0:T(8,128)(2,1)S(1)}, bf16[4,128,256]{2,1,0:T(8,128)(2,1)S(1)}, u32[]{:S(2)}, u32[]{:S(2)}) collective-permute-start(bf16[4,128,256]{2,1,0:T(8,128)(2,1)S(1)} %collective-permute-done.3.refs_4_), channel_id=1, source_target_pairs={{0,2},{1,3},{2,0},{3,1},{4,6},{5,7},{6,4},{7,5},{8,10},{9,11},{10,... | collective-permute-start | bytes 786440 | tf_op jit(solution)/shard_map/ppermute | solution.py:105
  16.6 10.7 %collective-permute-start.2 = (bf16[4,128,256]{2,1,0:T(8,128)(2,1)}, bf16[4,128,256]{2,1,0:T(8,128)(2,1)S(1)}, u32[]{:S(2)}, u32[]{:S(2)}) collective-permute-start(bf16[4,128,256]{2,1,0:T(8,128)(2,1)} %mask_strip.1.refs_0_), channel_id=1, source_target_pairs={{0,12},{4,0},{8,4},{12,8},{1,13},{5,1},{9,5},{13,9},{2,14},{6,2},{... | collective-permute-start | bytes 786440 | tf_op jit(solution)/shard_map/ppermute | solution.py:105
  20.2 21.4 %collective-permute-start.1 = (bf16[4,128,256]{2,1,0:T(8,128)(2,1)}, bf16[4,128,256]{2,1,0:T(8,128)(2,1)S(1)}, u32[]{:S(2)}, u32[]{:S(2)}) collective-permute-start(bf16[4,128,256]{2,1,0:T(8,128)(2,1)} %mask_strip.1.refs_0_), channel_id=1, source_target_pairs={{0,8},{4,12},{8,0},{12,4},{1,9},{5,13},{9,1},{13,5},{2,10},{6,14},... | collective-permute-start | bytes 786440 | tf_op jit(solution)/shard_map/ppermute | solution.py:105
  20.2 21.4 %collective-permute-start = (bf16[4,128,256]{2,1,0:T(8,128)(2,1)}, bf16[4,128,256]{2,1,0:T(8,128)(2,1)S(1)}, u32[]{:S(2)}, u32[]{:S(2)}) collective-permute-start(bf16[4,128,256]{2,1,0:T(8,128)(2,1)} %mask_strip.1.refs_0_), channel_id=1, source_target_pairs={{0,4},{4,8},{8,12},{12,0},{1,5},{5,9},{9,13},{13,1},{2,6},{6,10},{... | collective-permute-start | bytes 786440 | tf_op jit(solution)/shard_map/ppermute | solution.py:105
  21.2 20.4 %collective-permute-start.4 = (bf16[4,128,256]{2,1,0:T(8,128)(2,1)S(1)}, bf16[4,128,256]{2,1,0:T(8,128)(2,1)S(1)}, u32[]{:S(2)}, u32[]{:S(2)}) collective-permute-start(bf16[4,128,256]{2,1,0:T(8,128)(2,1)S(1)} %collective-permute-done.3.refs_4_), channel_id=1, source_target_pairs={{0,1},{1,0},{2,3},{3,2},{4,5},{5,4},{6,7},{7,6},{8,9},{9,8},{10,11... | collective-permute-start | bytes 786440 | tf_op jit(solution)/shard_map/ppermute | solution.py:105
  22.3 19.3 %collective-permute-start.6 = (bf16[4,128,256]{2,1,0:T(8,128)(2,1)S(1)}, bf16[4,128,256]{2,1,0:T(8,128)(2,1)S(1)}, u32[]{:S(2)}, u32[]{:S(2)}) collective-permute-start(bf16[4,128,256]{2,1,0:T(8,128)(2,1)S(1)} %collective-permute-done.5.refs_6_), channel_id=1, source_target_pairs={{0,1},{1,0},{2,3},{3,2},{4,5},{5,4},{6,7},{7,6},{8,9},{9,8},{10,11... | collective-permute-start | bytes 786440 | tf_op jit(solution)/shard_map/ppermute | solution.py:105
  41.6 1.0 %copy-start.2 = (bf16[4,128,256]{2,1,0:T(8,128)(2,1)S(1)}, bf16[4,128,256]{2,1,0:T(8,128)(2,1)}, u32[]{:S(2)}) copy-start(bf16[4,128,256]{2,1,0:T(8,128)(2,1)} %mask_strip.1.refs_0_) | copy-start | bytes 786436
